TPU v7x, 32 devices: a whole 2x2x4 slice. The times are simulated.
32 devices in a mesh: groups: 2 (over x), tiles: 16 (over z, y, core).
Axes of the slice: x: 2, y: 2, z: 4, core: 2. Of those that a mesh axis runs over, the one named last changes fastest.
Arguments:
- features: bfloat16 [512, 128, 128], P(('groups', 'tiles')), parts along dimension 0, may hold values from -40 to 40
- window_offsets: int32 [4], P('groups'), parts along dimension 0, may hold values from 0 to 31
- self_project: bfloat16 [128, 384], replicated, may hold values from -0.5 to 0.5
- self_merge: bfloat16 [128, 128], replicated, may hold values from -0.5 to 0.5
- cross_project: bfloat16 [128, 384], replicated, may hold values from -0.5 to 0.5
- cross_merge: bfloat16 [128, 128], replicated, may hold values from -0.5 to 0.5
- feed_in: bfloat16 [256, 512], replicated, may hold values from -0.375 to 0.375
- feed_out: bfloat16 [512, 128], replicated, may hold values from -0.25 to 0.25
- norm_gains: float32 [3, 128], replicated, may hold values from 0.1 to 1.9
- result_grad: float32 [512, 128, 128], P(('groups', 'tiles')), parts along dimension 0, may hold values from -6 to 6
Outputs:
- result: bfloat16 [512, 128, 128], P(('groups', 'tiles')), parts along dimension 0
- features_grad: float32 [512, 128, 128], P(('groups', 'tiles')), parts along dimension 0
- self_project_grad: float32 [256, 384], P(('groups', 'tiles')), parts along dimension 0
- self_merge_grad: float32 [256, 128], P(('groups', 'tiles')), parts along dimension 0
- cross_project_grad: float32 [256, 384], P(('groups', 'tiles')), parts along dimension 0
- cross_merge_grad: float32 [256, 128], P(('groups', 'tiles')), parts along dimension 0
- feed_in_grad: float32 [512, 512], P(('groups', 'tiles')), parts along dimension 0
- feed_out_grad: float32 [1024, 128], P(('groups', 'tiles')), parts along dimension 0
- norm_gains_grad: float32 [6, 128], P('groups', 'tiles'), parts along dimension 0
There are 2 independent parts, one for each index of `groups`. A program takes and returns all parts, laid end to end along the dimension named above; an argument that names none is the same for every part. Nothing has to cross between parts.
All inputs are finite; a program needn't handle non-finite values.
Results may differ from a plain program's by a relative error of at most 0.017.
The roundings to bfloat16 on the way count: a program that leaves them out, or rounds other values in their place, can miss the bound.
Values may be sent and summed in bfloat16 or wider, within the bound.
A program may use at most 128 MiB of HBM per device.

v0:
```python
import math

import jax
import jax.numpy as jnp
from jax import lax
from jax.sharding import PartitionSpec as P

D = 128
WIN = 32


NORM_EPS = 1e-05
MASK_FILL = -1000000000.0
HALF_ROOT = 0.7071067811865476
DENSITY_COEF = 0.3989422804014327


def extended_2(cells, sides, width):
    for axis, dim in sides:
        count = lax.axis_size(axis)
        head = lax.slice_in_dim(cells, 0, width, axis=dim)
        tail = lax.slice_in_dim(cells, cells.shape[dim] - width, cells.shape[dim], axis=dim)
        cells = jnp.concatenate(
            [
                lax.ppermute(tail, axis, [(i, (i + 1) % count) for i in range(count)]),
                cells,
                lax.ppermute(head, axis, [((i + 1) % count, i) for i in range(count)]),
            ],
            axis=dim,
        )
    return cells


def passed_along(array, axis, by):
    length = lax.axis_size(axis)
    return lax.ppermute(array, axis, [(i, (i + by) % length) for i in range(length)])


def project(inputs, weight):
    return lax.dot_general(
        inputs, weight, (((1,), (0,)), ((), ())), preferred_element_type=jnp.float32
    )


def back_project(grad_rows, weight):
    return lax.dot_general(
        grad_rows, weight, (((1,), (1,)), ((), ())), preferred_element_type=jnp.float32
    )


def weight_grad(inputs, grad_rows):
    return lax.dot_general(
        inputs, grad_rows, (((0,), (0,)), ((), ())), preferred_element_type=jnp.float32
    )


def layer_norm(values, norm_gain):
    center = values - jnp.mean(values, axis=-1, keepdims=True)
    inverse = lax.rsqrt(jnp.mean(center * center, axis=-1, keepdims=True) + NORM_EPS)
    unit_rows = center * inverse
    return (unit_rows * norm_gain, unit_rows, inverse)


def norm_backward(upstream, norm_gain, unit_rows, inverse):
    scaled = upstream * norm_gain
    value_gradient = inverse * (
        scaled
        - jnp.mean(scaled, axis=-1, keepdims=True)
        - unit_rows * jnp.mean(scaled * unit_rows, axis=-1, keepdims=True)
    )
    return (value_gradient, jnp.sum(upstream * unit_rows, axis=0))


def gelu_exact(values):
    return 0.5 * values * (1.0 + lax.erf(values * HALF_ROOT))


def gelu_slope(values):
    return (
        0.5 * (1.0 + lax.erf(values * HALF_ROOT))
        + values * jnp.exp(-0.5 * values * values) * DENSITY_COEF
    )


def to_windows(array, row_groups, group_rows, col_groups):
    width = array.shape[-1]
    shaped = array.reshape(row_groups, group_rows, col_groups, WIN, width)
    return shaped.transpose(0, 2, 1, 3, 4).reshape(row_groups * col_groups, group_rows * WIN, width)


def from_windows(array, row_groups, group_rows, col_groups):
    width = array.shape[-1]
    shaped = array.reshape(row_groups, col_groups, group_rows, WIN, width)
    return shaped.transpose(0, 2, 1, 3, 4).reshape(row_groups * group_rows, col_groups * WIN, width)


def attention_shares(query_rows, key_matrix, key_valid, logit_scale):
    attention_logits = (
        jnp.einsum("hcn,hzn->hcz", query_rows, key_matrix, preferred_element_type=jnp.float32)
        * logit_scale
    )
    attention_logits = jnp.where(key_valid, attention_logits, MASK_FILL)
    top_score = jnp.max(attention_logits, axis=-1, keepdims=True)
    raised = jnp.exp(attention_logits - top_score)
    shares = raised / jnp.sum(raised, axis=-1, keepdims=True)
    return (shares, shares.astype(jnp.bfloat16))


def apply_shares(portion_weights, value_matrix):
    return jnp.einsum(
        "tni,tip->tnp", portion_weights, value_matrix, preferred_element_type=jnp.float32
    ).astype(jnp.bfloat16)


def shares_backward(
    query_rows, key_matrix, value_matrix, shares, portion_weights, mixture_gradient, logit_scale
):
    portion_gradient = jnp.einsum(
        "hcn,hzn->hcz", mixture_gradient, value_matrix, preferred_element_type=jnp.float32
    )
    value_gradient = jnp.einsum(
        "nvw,nvc->nwc", portion_weights, mixture_gradient, preferred_element_type=jnp.float32
    )
    inner_sum = jnp.sum(portion_gradient * shares, axis=-1, keepdims=True)
    logit_gradient = (shares * (portion_gradient - inner_sum) * logit_scale).astype(jnp.bfloat16)
    query_gradient = jnp.einsum(
        "tni,tip->tnp", logit_gradient, key_matrix, preferred_element_type=jnp.float32
    )
    key_gradient = jnp.einsum(
        "nvw,nvc->nwc", logit_gradient, query_rows, preferred_element_type=jnp.float32
    )
    return (query_gradient, key_gradient, value_gradient)


def body(
    features,
    window_offsets,
    self_project,
    self_merge,
    cross_project,
    cross_merge,
    feed_in,
    feed_out,
    norm_gains,
    result_grad,
):
    tile_rows = features.shape[0]
    tile_cols = features.shape[1]
    half_rows = tile_rows // 2
    tile_tokens = tile_rows * tile_cols
    col_groups = tile_cols // WIN
    tiles_count = lax.axis_size("tiles")
    half_tiles = tiles_count // 2
    position = lax.axis_index("tiles")
    image_place = (position + tiles_count - tiles_count // 4) % tiles_count
    offset = window_offsets[image_place // half_tiles]
    logit_scale = D ** (-0.5)
    grad_scale = 1.0 / math.sqrt(tiles_count * tile_tokens)
    upper_valid = image_place % half_tiles != 0
    lower_valid = image_place % half_tiles != half_tiles - 1
    rolled = jnp.roll(features, -offset, axis=1)
    rolled_flat = rolled.reshape(tile_tokens, D)
    self_proj = (
        project(rolled_flat, self_project).astype(jnp.bfloat16).reshape(tile_rows, tile_cols, 3 * D)
    )
    extended = extended_2(self_proj[:, :, D:], (("tiles", 0),), half_rows)
    window_queries = to_windows(self_proj[:, :, :D], 2, half_rows, col_groups)
    window_keyval = to_windows(extended, 2, tile_rows, col_groups)
    row_flags = jnp.concatenate(
        [
            jnp.full((half_rows,), upper_valid),
            jnp.full((tile_rows,), True),
            jnp.full((half_rows,), lower_valid),
        ]
    )
    key_valid = jnp.broadcast_to(
        row_flags.reshape(2, 1, tile_rows, 1), (2, col_groups, tile_rows, WIN)
    ).reshape(2 * col_groups, 1, tile_rows * WIN)
    self_shares, self_weights = attention_shares(
        window_queries, window_keyval[:, :, :D], key_valid, logit_scale
    )
    window_mix = apply_shares(self_weights, window_keyval[:, :, D:])
    rolled_mix = from_windows(window_mix, 2, half_rows, col_groups)
    self_mix = jnp.roll(rolled_mix, offset, axis=1).reshape(tile_tokens, D)
    self_normed, self_unit, self_inverse = layer_norm(project(self_mix, self_merge), norm_gains[0])
    middle = (features.reshape(tile_tokens, D).astype(jnp.float32) + self_normed).astype(
        jnp.bfloat16
    )
    cross_query = project(middle, cross_project[:, :D]).astype(jnp.bfloat16)
    keyval_weight = cross_project[:, D:]
    partner_middle = passed_along(middle, "tiles", half_tiles)
    partner_keyval = project(partner_middle, keyval_weight).astype(jnp.bfloat16)
    block_rows = min(512, tile_tokens)
    block_count = tile_tokens // block_rows
    query_blocks = cross_query.reshape(block_count, block_rows, D)
    partner_keys = partner_keyval[None, :, :D]
    partner_values = partner_keyval[None, :, D:]
    all_valid = jnp.full((1, 1, tile_tokens), True)

    def cross_block(query_block):
        shares, weights = attention_shares(query_block[None], partner_keys, all_valid, logit_scale)
        return apply_shares(weights, partner_values)[0]

    cross_mix = lax.map(cross_block, query_blocks).reshape(tile_tokens, D)
    cross_full, cross_unit, cross_inverse = layer_norm(
        project(cross_mix, cross_merge), norm_gains[1]
    )
    cross_normed = cross_full.astype(jnp.bfloat16)
    joined = jnp.concatenate([middle, cross_normed], axis=1)
    feed_pre = project(joined, feed_in)
    feed_hidden = gelu_exact(feed_pre).astype(jnp.bfloat16)
    feed_normed, feed_unit, feed_inverse = layer_norm(project(feed_hidden, feed_out), norm_gains[2])
    result = (middle.astype(jnp.float32) + feed_normed).astype(jnp.bfloat16)
    upstream = result_grad.reshape(tile_tokens, D)
    grad_post_full, gain_feed = norm_backward(upstream, norm_gains[2], feed_unit, feed_inverse)
    grad_post = grad_post_full.astype(jnp.bfloat16)
    grad_pre = (back_project(grad_post, feed_out) * gelu_slope(feed_pre)).astype(jnp.bfloat16)
    grad_joined = back_project(grad_pre, feed_in)
    grad_feed_in = weight_grad(joined, grad_pre) * grad_scale
    grad_feed_out = weight_grad(feed_hidden, grad_post) * grad_scale
    gain_feed = gain_feed * grad_scale
    grad_cross_full, gain_cross = norm_backward(
        grad_joined[:, D:], norm_gains[1], cross_unit, cross_inverse
    )
    grad_cross_merged = grad_cross_full.astype(jnp.bfloat16)
    grad_cross_merge = weight_grad(cross_mix, grad_cross_merged) * grad_scale
    grad_cross_mix = back_project(grad_cross_merged, cross_merge).astype(jnp.bfloat16)
    mix_grad_blocks = grad_cross_mix.reshape(block_count, block_rows, D)

    def cross_block_back(carry, pieces):
        query_block, mix_grad_block = pieces
        shares, weights = attention_shares(query_block[None], partner_keys, all_valid, logit_scale)
        query_gradient, key_gradient, value_gradient = shares_backward(
            query_block[None],
            partner_keys,
            partner_values,
            shares,
            weights,
            mix_grad_block[None],
            logit_scale,
        )
        return ((carry[0] + key_gradient[0], carry[1] + value_gradient[0]), query_gradient[0])

    empty_rows = jnp.zeros((tile_tokens, D), jnp.float32)
    (partner_grad_keys, partner_grad_values), grad_query_blocks = lax.scan(
        cross_block_back, (empty_rows, empty_rows), (query_blocks, mix_grad_blocks)
    )
    grad_cross_query = grad_query_blocks.reshape(tile_tokens, D).astype(jnp.bfloat16)
    grad_partner_keyval = jnp.concatenate([partner_grad_keys, partner_grad_values], axis=1).astype(
        jnp.bfloat16
    )
    grad_middle = (
        upstream + grad_joined[:, :D] + back_project(grad_cross_query, cross_project[:, :D])
    )
    query_weight_grad = weight_grad(middle, grad_cross_query)
    partner_term = back_project(grad_partner_keyval, keyval_weight)
    grad_middle = grad_middle + passed_along(partner_term, "tiles", half_tiles)
    keyval_weight_grad = weight_grad(partner_middle, grad_partner_keyval)
    grad_cross_project = (
        jnp.concatenate([query_weight_grad, keyval_weight_grad], axis=1) * grad_scale
    )
    gain_cross = gain_cross * grad_scale
    grad_self_full, gain_self = norm_backward(grad_middle, norm_gains[0], self_unit, self_inverse)
    grad_self_merged = grad_self_full.astype(jnp.bfloat16)
    grad_self_merge = weight_grad(self_mix, grad_self_merged) * grad_scale
    grad_self_mix = (
        back_project(grad_self_merged, self_merge)
        .astype(jnp.bfloat16)
        .reshape(tile_rows, tile_cols, D)
    )
    rolled_grad = jnp.roll(grad_self_mix, -offset, axis=1)
    window_mix_grad = to_windows(rolled_grad, 2, half_rows, col_groups)
    window_grad_query, window_grad_keys, window_grad_values = shares_backward(
        window_queries,
        window_keyval[:, :, :D],
        window_keyval[:, :, D:],
        self_shares,
        self_weights,
        window_mix_grad,
        logit_scale,
    )
    grad_extended = from_windows(
        jnp.concatenate([window_grad_keys, window_grad_values], axis=2), 2, tile_rows, col_groups
    )
    from_upper = passed_along(grad_extended[tile_rows + half_rows :], "tiles", 1)
    from_lower = passed_along(grad_extended[:half_rows], "tiles", -1)
    from_upper = jnp.where(upper_valid, from_upper, jnp.zeros_like(from_upper))
    from_lower = jnp.where(lower_valid, from_lower, jnp.zeros_like(from_lower))
    own_grad_keyval = grad_extended[half_rows : half_rows + tile_rows] + jnp.concatenate(
        [from_upper, from_lower], axis=0
    )
    grad_self_proj = (
        jnp.concatenate(
            [from_windows(window_grad_query, 2, half_rows, col_groups), own_grad_keyval], axis=2
        )
        .astype(jnp.bfloat16)
        .reshape(tile_tokens, 3 * D)
    )
    grad_self_project = weight_grad(rolled_flat, grad_self_proj) * grad_scale
    rolled_term = back_project(grad_self_proj, self_project).reshape(tile_rows, tile_cols, D)
    rolled_back = jnp.roll(rolled_term, offset, axis=1)
    features_grad = grad_middle.reshape(tile_rows, tile_cols, D) + rolled_back
    gain_self = gain_self * grad_scale
    (
        summed_self_project,
        summed_self_merge,
        summed_cross_project,
        summed_cross_merge,
        summed_feed_in,
        summed_feed_out,
        summed_gain_self,
        summed_gain_cross,
        summed_gain_feed,
    ) = (
        lax.psum_scatter(grad_self_project, "tiles", scatter_dimension=0, tiled=True),
        lax.psum_scatter(grad_self_merge, "tiles", scatter_dimension=0, tiled=True),
        lax.psum_scatter(grad_cross_project, "tiles", scatter_dimension=0, tiled=True),
        lax.psum_scatter(grad_cross_merge, "tiles", scatter_dimension=0, tiled=True),
        lax.psum_scatter(grad_feed_in, "tiles", scatter_dimension=0, tiled=True),
        lax.psum_scatter(grad_feed_out, "tiles", scatter_dimension=0, tiled=True),
        lax.psum_scatter(gain_self[None], "tiles", scatter_dimension=1, tiled=True),
        lax.psum_scatter(gain_cross[None], "tiles", scatter_dimension=1, tiled=True),
        lax.psum_scatter(gain_feed[None], "tiles", scatter_dimension=1, tiled=True),
    )
    summed_gains = jnp.concatenate([summed_gain_self, summed_gain_cross, summed_gain_feed], axis=0)
    return (
        result.reshape(tile_rows, tile_cols, D),
        features_grad,
        summed_self_project,
        summed_self_merge,
        summed_cross_project,
        summed_cross_merge,
        summed_feed_in,
        summed_feed_out,
        summed_gains,
    )


def solution(mesh):
    return jax.shard_map(
        body,
        mesh=mesh,
        in_specs=(
            P(("groups", "tiles"), None, None),
            P("groups"),
            P(),
            P(),
            P(),
            P(),
            P(),
            P(),
            P(),
            P(("groups", "tiles"), None, None),
        ),
        out_specs=(
            P(("groups", "tiles"), None, None),
            P(("groups", "tiles"), None, None),
            P(("groups", "tiles"), None),
            P(("groups", "tiles"), None),
            P(("groups", "tiles"), None),
            P(("groups", "tiles"), None),
            P(("groups", "tiles"), None),
            P(("groups", "tiles"), None),
            P("groups", "tiles"),
        ),
        check_vma=False,
    )
```

profile of v0, /device:TPU:0, one launch (start us, length us, event | category | flops | bytes accessed | tf_op | source)
XLA Modules:
  0.0 488.0 jit_solution(18295183460158121471)
XLA Ops:
  14.9 5.0 %collective-permute-start.1 = (bf16[8,128,256]{2,1,0:T(8,128)(2,1)}, bf16[8,128,256]{2,1,0:T(8,128)(2,1)}, u32[]{:S(2)}, u32[]{:S(2)}) collective-permute-start(bf16[8,128,256]{2,1,0:T(8,128)(2,1)} %get-tuple-element.162), channel_id=1, source_target_pairs={{1,0},{2,1},{3,2},{4,3},{5,4},{6,5},{7,6},{8,7},{9,8},{10,9},{11,1... | collective-permute-start | bytes 1572872 | tf_op jit(solution)/shard_map/ppermute | solution.py:27
  23.7 3.5 collective-permute-done
  29.6 2.3 fusion.103
  39.1 23.7 %collective-permute-done.2 = bf16[2048,128]{1,0:T(8,128)(2,1)S(1)} collective-permute-done((bf16[2048,128]{1,0:T(8,128)(2,1)S(1)}, bf16[2048,128]{1,0:T(8,128)(2,1)S(1)}, u32[]{:S(2)}, u32[]{:S(2)}) %collective-permute-start.2) | collective-permute-done | bytes 524320 | tf_op jit(solution)/shard_map/ppermute | solution.py:36
  64.9 17.0 %while.25 = (s32[]{:T(128)}, bf16[4,512,128]{2,1,0:T(8,128)(2,1)}, bf16[4,512,128]{2,1,0:T(8,128)(2,1)}, bf16[1,2048,128]{2,1,0:T(8,128)(2,1)S(1)}, bf16[1,2048,128]{2,1,0:T(8,128)(2,1)}, /*index=5*/s32[]{:T(128)}) while((s32[]{:T(128)}, bf16[4,512,128]{2,1,0:T(8,128)(2,1)}, bf16[4,512,128]{2,1,0:T(8,128)(2,1)}, ...), condition=%wide.region_7.9_spmd, body=%wide.region_4.8_spmd.sunk | while | flops 546372608 | bytes 16001137 | solution.py:204
  81.9 2.4 fusion.105
  84.2 2.5 copy.49
  86.8 1.9 multiply_reduce_fusion.11
  94.1 2.5 multiply_convert_fusion.5
  96.6 2.1 fusion.41
  105.0 41.5 %while.26 = (s32[]{:T(128)}, f32[2048,128]{1,0:T(8,128)S(1)}, f32[2048,128]{1,0:T(8,128)}, bf16[4,512,128]{2,1,0:T(8,128)(2,1)}, bf16[4,512,128]{2,1,0:T(8,128)(...) while((s32[]{:T(128)}, f32[2048,128]{1,0:T(8,128)S(1)}, ...), condition=%wide.region_20.22_spmd.clone, body=%wide.region_16.21_spmd.clone.sunk | while | flops 1365244416 | bytes 59005232 | solution.py:245
  113.2 2.1 convolution_add_fusion.5
  123.6 2.1 convolution_add_fusion.5
  134.0 2.1 convolution_add_fusion.5
  144.3 2.1 convolution_add_fusion.5
  148.9 48.0 %collective-permute-done.3 = f32[2048,128]{1,0:T(8,128)S(1)} collective-permute-done((f32[2048,128]{1,0:T(8,128)S(1)}, f32[2048,128]{1,0:T(8,128)S(1)}, u32[]{:S(2)}, u32[]{:S(2)}) %collective-permute-start.3) | collective-permute-done | bytes 1048608 | tf_op jit(solution)/shard_map/ppermute | solution.py:36
  198.2 1.9 multiply_convert_fusion.3
  201.0 2.1 fusion.67
  203.0 2.7 fusion.71
  205.7 19.2 %fusion.47 = f32[8,512,128]{1,2,0:T(8,128)} fusion(bf16[8,256,128]{2,1,0:T(8,128)(2,1)} %bitcast.219, f32[8,256,512]{2,1,0:T(8,128)} %fusion.71, f32[8,256,512]{2,1,0:T(8,128)} %copy-done.54, f32[8,256]{1,0:T(8,128)S(1)} %copy-done.57), kind=kOutput, calls=%fused_computation.63 | convolution fusion | flops 275778048 | bytes 11018240 | tf_op jit(solution)/shard_map/nvw,nvc->nwc/dot_general | solution.py:129
  224.9 4.6 pad_maximum_fusion
  229.5 5.3 %copy.54 = f32[8,512,256]{2,1,0:T(8,128)} copy(f32[8,512,256]{1,2,0:T(8,128)} %pad_maximum_fusion) | data formatting | bytes 8388608 | tf_op jit(solution)/shard_map/concatenate | solution.py:283
  234.9 2.5 copy.55
  237.4 2.1 copy-done.7
  241.5 4.5 collective-permute-start.5
  247.7 17.5 %fusion.59 = bf16[8,256,128]{2,1,0:T(8,128)(2,1)} fusion(f32[8,256,512]{2,1,0:T(8,128)} %fusion.71, bf16[8,512,256]{2,1,0:T(8,128)(2,1)S(1)} %bitcast.206, f32[8,256,512]{2,1,0:T(8,128)} %copy-done.54, f32[8,256]{1,0:T(8,128)S(1)} %copy-done.57), kind=kOutput, calls=%fused_computation.82 | convolution fusion | flops 276040192 | bytes 18366464 | tf_op jit(solution)/shard_map/tni,tip->tnp/dot_general | solution.py:126
  266.4 2.4 convolution_multiply_fusion.3
  276.9 3.4 convolution_multiply_fusion
  280.3 29.6 %all-reduce.7 = (f32[1,128]{1,0:T(1,128)S(1)}, f32[1,128]{1,0:T(1,128)S(1)}, f32[1,128]{1,0:T(1,128)S(1)}) all-reduce(f32[1,128]{1,0:T(1,128)S(1)} %get-tuple-element.183, f32[1,128]{1,0:T(1,128)S(1)} %get-tuple-element.184, f32[1,128]{1,0:T(1,128)S(1)} %multiply_bitcast_fusion.3), channel_id=10, replica_groups=mesh['groups'=2,'tiles'=16] {'tiles'}, use_global_device_ids=true, to_apply=%region_35.37.clone | all-reduce | flops 384 | bytes 3072
  312.6 49.4 %all-reduce.11.cloned.1.call-done = (f32[128,384]{1,0:T(8,128)}, f32[128,128]{1,0:T(8,128)}, f32[128,384]{1,0:T(8,128)}, f32[128,128]{1,0:T(8,128)}) async-done(((f32[128,384]{1,0:T(8,128)}, f32[128,128]{1,0:T(8,128)}, f32[128,384]{1,0:T(8,128)}, f32[128,128]{1,0:T(8,128)}), (f32[128,384]{1,0:T(8,128)}, f32[128,128]{1,0:T(8,128)}, f32[128,384]{1,0:T(8,128)}, ...) | async-done | bytes 524304
  367.2 54.8 %reduce-scatter.8.cloned.1.call-done = f32[32,128]{1,0:T(8,128)} async-done(((f32[512,128]{1,0:T(8,128)}), f32[32,128]{1,0:T(8,128)}) %reduce-scatter.8.cloned.1.call-update) | async-done | bytes 16400 | tf_op jit(solution)/shard_map/reduce_scatter | solution.py:320
  422.0 59.0 %reduce-scatter.6.cloned.1.call-done = f32[16,512]{1,0:T(8,128)} async-done(((f32[256,512]{1,0:T(8,128)}), f32[16,512]{1,0:T(8,128)}) %reduce-scatter.6.cloned.1.call-update) | async-done | bytes 32784 | tf_op jit(solution)/shard_map/reduce_scatter | solution.py:319
  (291 shorter events, 105.9 us)
Async XLA Ops:
  7.2 83.3 %copy-start = (bf16[256,512]{1,0:T(8,128)(2,1)S(1)}, bf16[256,512]{1,0:T(8,128)(2,1)}, u32[]{:S(2)}) copy-start(bf16[256,512]{1,0:T(8,128)(2,1)} %param.22) | copy-start | bytes 786436
  7.2 354.9 %all-reduce.11.cloned.1.call-start = ((), (), s32[]{:S(2)}) async-start(), calls=%async_computation.4 | async-start | bytes 1048576
  11.6 10.6 %copy-start.27 = (bf16[16,128,128]{1,2,0:T(8,128)(2,1)}, bf16[16,128,128]{1,2,0:T(8,128)(2,1)S(1)}, u32[]{:S(2)}) copy-start(bf16[16,128,128]{1,2,0:T(8,128)(2,1)S(1)} %fusion.83) | copy-start | bytes 1572868
  11.9 11.8 %copy-start.52 = (f32[3,128]{1,0:T(4,128)S(1)}, f32[3,128]{1,0:T(4,128)}, u32[]{:S(2)}) copy-start(f32[3,128]{1,0:T(4,128)} %param.24) | copy-start | bytes 4612
  14.4 12.7 %collective-permute-start = (bf16[8,128,256]{2,1,0:T(8,128)(2,1)}, bf16[8,128,256]{2,1,0:T(8,128)(2,1)}, u32[]{:S(2)}, u32[]{:S(2)}) collective-permute-start(bf16[8,128,256]{2,1,0:T(8,128)(2,1)} %get-tuple-element.161), channel_id=1, source_target_pairs={{0,1},{1,2},{2,3},{3,4},{4,5},{5,6},{6,7},{7,8},{8,9},{9,10},{10,1... | collective-permute-start | bytes 1572872 | tf_op jit(solution)/shard_map/ppermute | solution.py:25
  14.9 12.3 %collective-permute-start.1 = (bf16[8,128,256]{2,1,0:T(8,128)(2,1)}, bf16[8,128,256]{2,1,0:T(8,128)(2,1)}, u32[]{:S(2)}, u32[]{:S(2)}) collective-permute-start(bf16[8,128,256]{2,1,0:T(8,128)(2,1)} %get-tuple-element.162), channel_id=1, source_target_pairs={{1,0},{2,1},{3,2},{4,3},{5,4},{6,5},{7,6},{8,7},{9,8},{10,9},{11,1... | collective-permute-start | bytes 1572872 | tf_op jit(solution)/shard_map/ppermute | solution.py:27
  23.7 5.2 %copy-start.33 = (bf16[2,8,4,32,128]{4,3,1,2,0:T(8,128)(2,1)}, bf16[2,8,4,32,128]{4,3,1,2,0:T(8,128)(2,1)S(1)}, u32[]{:S(2)}) copy-start(bf16[2,8,4,32,128]{4,3,1,2,0:T(8,128)(2,1)S(1)} %copy.46) | copy-start | bytes 1572868
  33.8 3.7 copy-start.9
  33.8 4.1 copy-start.46
  36.3 26.5 %collective-permute-start.2 = (bf16[2048,128]{1,0:T(8,128)(2,1)S(1)}, bf16[2048,128]{1,0:T(8,128)(2,1)S(1)}, u32[]{:S(2)}, u32[]{:S(2)}) collective-permute-start(bf16[2048,128]{1,0:T(8,128)(2,1)S(1)} %fusion.65), channel_id=1, source_target_pairs={{0,8},{1,9},{2,10},{3,11},{4,12},{5,13},{6,14},{7,15},{8,0},{9,1},... | collective-permute-start | bytes 1572872 | tf_op jit(solution)/shard_map/ppermute | solution.py:36
  91.5 5.1 %copy-start.5 = (bf16[2048,512]{1,0:T(8,128)(2,1)}, bf16[2048,512]{1,0:T(8,128)(2,1)S(1)}, u32[]{:S(2)}) copy-start(bf16[2048,512]{1,0:T(8,128)(2,1)S(1)} %get-tuple-element.176) | copy-start | bytes 6291460
  146.5 50.4 %copy-start.4 = (f32[2048,256]{1,0:T(8,128)S(1)}, f32[2048,256]{1,0:T(8,128)}, u32[]{:S(2)}) copy-start(f32[2048,256]{1,0:T(8,128)} %copy-done.3) | copy-start | bytes 6291460
  146.5 50.4 %copy-start.11 = (f32[16,128,128]{2,1,0:T(8,128)S(1)}, f32[16,128,128]{2,1,0:T(8,128)}, u32[]{:S(2)}) copy-start(f32[16,128,128]{2,1,0:T(8,128)} %param.25) | copy-start | bytes 3145732
  148.0 48.9 %copy-start.29 = (bf16[2048,128]{1,0:T(8,128)(2,1)}, bf16[2048,128]{1,0:T(8,128)(2,1)S(1)}, u32[]{:S(2)}) copy-start(bf16[2048,128]{1,0:T(8,128)(2,1)S(1)} %convert.17) | copy-start | bytes 1572868
  148.4 48.4 %collective-permute-start.3 = (f32[2048,128]{1,0:T(8,128)S(1)}, f32[2048,128]{1,0:T(8,128)S(1)}, u32[]{:S(2)}, u32[]{:S(2)}) collective-permute-start(f32[2048,128]{1,0:T(8,128)S(1)} %fusion.79), channel_id=1, source_target_pairs={{0,8},{1,9},{2,10},{3,11},{4,12},{5,13},{6,14},{7,15},{8,0},{9,1},... | collective-permute-start | bytes 3145736 | tf_op jit(solution)/shard_map/ppermute | solution.py:36
  237.4 3.8 copy-start.30
  237.4 3.7 copy-start.40
  237.4 9.3 %copy-start.20 = (bf16[2048,128]{1,0:T(8,128)(2,1)S(1)}, bf16[2048,128]{1,0:T(8,128)(2,1)}, u32[]{:S(2)}) copy-start(bf16[2048,128]{1,0:T(8,128)(2,1)} %copy-done.19) | copy-start | bytes 1572868
  237.4 9.3 %copy-start.26 = (bf16[4,512,128]{2,1,0:T(8,128)(2,1)S(1)}, bf16[4,512,128]{2,1,0:T(8,128)(2,1)}, u32[]{:S(2)}) copy-start(bf16[4,512,128]{2,1,0:T(8,128)(2,1)} %get-tuple-element.81) | copy-start | bytes 1572868
  241.1 27.6 %collective-permute-start.4 = (f32[8,128,256]{2,1,0:T(8,128)}, f32[8,128,256]{2,1,0:T(8,128)}, u32[]{:S(2)}, u32[]{:S(2)}) collective-permute-start(f32[8,128,256]{2,1,0:T(8,128)} %get-tuple-element.159), channel_id=1, source_target_pairs={{0,1},{1,2},{2,3},{3,4},{4,5},{5,6},{6,7},{7,8},{8,9},{9,10},{10,1... | collective-permute-start | bytes 3145736 | tf_op jit(solution)/shard_map/ppermute | solution.py:36
  241.5 28.5 %collective-permute-start.5 = (f32[8,128,256]{2,1,0:T(8,128)}, f32[8,128,256]{2,1,0:T(8,128)}, u32[]{:S(2)}, u32[]{:S(2)}) collective-permute-start(f32[8,128,256]{2,1,0:T(8,128)} %get-tuple-element.160), channel_id=1, source_target_pairs={{0,15},{1,0},{2,1},{3,2},{4,3},{5,4},{6,5},{7,6},{8,7},{9,8},{10,9... | collective-permute-start | bytes 3145736 | tf_op jit(solution)/shard_map/ppermute | solution.py:36
  247.7 18.7 %copy-start.18 = (bf16[16,128,128]{2,1,0:T(8,128)(2,1)S(1)}, bf16[16,128,128]{2,1,0:T(8,128)(2,1)}, u32[]{:S(2)}) copy-start(bf16[16,128,128]{2,1,0:T(8,128)(2,1)} %copy-done.17) | copy-start | bytes 1572868
  265.1 6.3 %copy-start.8 = (f32[2,16,4,32,256]{4,3,2,1,0:T(8,128)S(1)}, f32[2,16,4,32,256]{4,3,2,1,0:T(8,128)}, u32[]{:S(2)}) copy-start(f32[2,16,4,32,256]{4,3,2,1,0:T(8,128)} %copy-done.7) | copy-start | bytes 12582916
  266.4 5.6 %copy-start.41 = (bf16[2,8,4,32,128]{4,3,2,1,0:T(8,128)(2,1)}, bf16[2,8,4,32,128]{4,3,2,1,0:T(8,128)(2,1)S(1)}, u32[]{:S(2)}) copy-start(bf16[2,8,4,32,128]{4,3,2,1,0:T(8,128)(2,1)S(1)} %copy.51) | copy-start | bytes 1572868
  271.9 3.7 copy-start.53
  274.0 36.7 %copy-start.51 = (bf16[128,384]{1,0:T(8,128)(2,1)S(1)}, bf16[128,384]{1,0:T(8,128)(2,1)}, u32[]{:S(2)}) copy-start(bf16[128,384]{1,0:T(8,128)(2,1)} %param.18) | copy-start | bytes 294916
  274.0 148.0 %reduce-scatter.8.cloned.1.call-start = ((), (), s32[]{:S(2)}) async-start(), calls=%async_computation.3 | async-start | bytes 278528 | tf_op jit(solution)/shard_map/reduce_scatter | solution.py:320
  275.5 35.2 %copy-start.36 = (bf16[16,128,256]{2,1,0:T(8,128)(2,1)S(1)}, bf16[16,128,256]{2,1,0:T(8,128)(2,1)}, u32[]{:S(2)}) copy-start(bf16[16,128,256]{2,1,0:T(8,128)(2,1)} %copy-done.35) | copy-start | bytes 3145732
  275.6 35.2 %copy-start.42 = (bf16[2,8,4,32,128]{4,3,2,1,0:T(8,128)(2,1)S(1)}, bf16[2,8,4,32,128]{4,3,2,1,0:T(8,128)(2,1)}, u32[]{:S(2)}) copy-start(bf16[2,8,4,32,128]{4,3,2,1,0:T(8,128)(2,1)} %copy-done.41) | copy-start | bytes 1572868
  275.6 205.4 %reduce-scatter.6.cloned.1.call-start = ((), (), s32[]{:S(2)}) async-start(), calls=%async_computation.2 | async-start | bytes 557056 | tf_op jit(solution)/shard_map/reduce_scatter | solution.py:319
  276.9 34.5 %copy-start.13 = (f32[2048,128]{1,0:T(8,128)S(1)}, f32[2048,128]{1,0:T(8,128)}, u32[]{:S(2)}) copy-start(f32[2048,128]{1,0:T(8,128)} %copy-done.12) | copy-start | bytes 3145732
  276.9 204.1 %copy-start.1 = (bf16[256,512]{1,0:T(8,128)(2,1)S(1)}, bf16[256,512]{1,0:T(8,128)(2,1)}, u32[]{:S(2)}) copy-start(bf16[256,512]{1,0:T(8,128)(2,1)} %param.22) | copy-start | bytes 786436
  (56 other events, 117.5 us)
Sparse Core Ops, SparseCore 0:
  274.1 87.8 all-reduce.10
  366.1 55.8 reduce-scatter.7
  426.1 54.8 reduce-scatter.5
where the time goes:
time: 492 us; the launch traced here: 488 us
  waiting for transfers between devices  238 us (48%)
  matrix products  112 us (23%)
  other arithmetic  44.1 us (9%)
  local copies, waits for them, and re-layouts  33.3 us (7%)
  blocking collectives  29.6 us (6%)
  between operations  18.5 us (4%)
  starting transfers between devices  11.4 us (2%)
    ppermute x4, waiting for transfers between devices, passed_along(): lax.ppermute(array, axis, [(i, (i + by) % length) for i in range(length)])  71.7 us
    reduce_scatter x1, waiting for transfers between devices, body(): lax.psum_scatter(grad_feed_in, 'tiles', scatter_dimension=0, tiled=True)  59 us
    reduce_scatter x1, waiting for transfers between devices, body(): lax.psum_scatter(grad_feed_out, 'tiles', scatter_dimension=0, tiled=True)  54.8 us
    unnamed x4, waiting for transfers between devices  49.5 us
    unnamed x1, blocking collectives  29.6 us
    dot_general x5, matrix products, shares_backward(): jnp.einsum('nvw,nvc->nwc', logit_gradient, query_rows, preferred_element_...  27.6 us
    dot_general x5, matrix products, shares_backward(): jnp.einsum('tni,tip->tnp', logit_gradient, key_matrix, preferred_element_...  20.6 us
    dot_general x9, matrix products, attention_shares(): jnp.einsum('hcn,hzn->hcz', query_rows, key_matrix, preferred_element_type...  14.9 us
  transfers between devices with their start and end apart: 9, of which 6 were waited for; matrix products, arithmetic and copies ran while one was open for 9% of the time, Pallas kernels for 0%

commit v1 on v0

v1 whole, which is shorter than its diff:
```python
import functools
import math

import jax
import jax.numpy as jnp
from jax import lax
from jax.experimental import pallas as pl
from jax.experimental.pallas import tpu as pltpu
from jax.sharding import PartitionSpec as P

WIN = 32
NORM_EPS = 1e-05
MASK_FILL = -1000000000.0
HALF_ROOT = 0.7071067811865476
DENSITY_COEF = 0.3989422804014327
VMEM_BYTES = 56 * 1024 * 1024
F32 = jnp.float32
BF16 = jnp.bfloat16


def passed_along(array, axis, by):
    length = lax.axis_size(axis)
    return lax.ppermute(array, axis, [(i, (i + by) % length) for i in range(length)])


def dot_nn(a, b):
    return lax.dot_general(a, b, (((1,), (0,)), ((), ())), preferred_element_type=F32)


def dot_nt(a, b):
    return lax.dot_general(a, b, (((1,), (1,)), ((), ())), preferred_element_type=F32)


def dot_tn(a, b):
    return lax.dot_general(a, b, (((0,), (0,)), ((), ())), preferred_element_type=F32)


def unit_norm(values):
    center = values - jnp.mean(values, axis=-1, keepdims=True)
    inverse = lax.rsqrt(jnp.mean(center * center, axis=-1, keepdims=True) + NORM_EPS)
    return center * inverse, inverse


def norm_backward(upstream, gain, unit_rows, inverse):
    scaled = upstream * gain
    return inverse * (
        scaled
        - jnp.mean(scaled, axis=-1, keepdims=True)
        - unit_rows * jnp.mean(scaled * unit_rows, axis=-1, keepdims=True)
    )


def softmax_rows(logits):
    raised = jnp.exp(logits - jnp.max(logits, axis=-1, keepdims=True))
    return raised * (1.0 / jnp.sum(raised, axis=-1, keepdims=True))


def window_keep(valid_ref, cols, own, tokens):
    group = pl.program_id(0) // cols
    flag = valid_ref[group]
    column = lax.broadcasted_iota(jnp.int32, (1, tokens), 1)
    return (column < own) | (flag > 0)


def self_forward_kernel(
    cols, valid_ref, own_ref, halo_ref, weight_ref, merge_ref, gains_ref, mix_ref, middle_ref
):
    d = own_ref.shape[1]
    count = own_ref.shape[0]
    own = own_ref[...]
    own_proj = dot_nn(own, weight_ref[...]).astype(BF16)
    halo_kv = dot_nn(halo_ref[...], weight_ref[:, d:]).astype(BF16)
    keys = jnp.concatenate([own_proj[:, d : 2 * d], halo_kv[:, :d]], axis=0)
    values = jnp.concatenate([own_proj[:, 2 * d :], halo_kv[:, d:]], axis=0)
    logits = dot_nt(own_proj[:, :d], keys) * d**-0.5
    logits = jnp.where(window_keep(valid_ref, cols, count, 2 * count), logits, MASK_FILL)
    weights = softmax_rows(logits).astype(BF16)
    mix = dot_nn(weights, values).astype(BF16)
    unit, _ = unit_norm(dot_nn(mix, merge_ref[...]))
    mix_ref[...] = mix
    middle_ref[...] = (own.astype(F32) + unit * gains_ref[0:1, :]).astype(BF16)


def cross_kernel(
    scale,
    middle_ref,
    partner_ref,
    upstream_ref,
    project_ref,
    merge_ref,
    feed_in_ref,
    feed_out_ref,
    gains_ref,
    result_ref,
    partial_ref,
    term_ref,
    g_project_ref,
    g_merge_ref,
    g_in_ref,
    g_out_ref,
    g_gain_ref,
    key_ref,
    value_ref,
    dkey_ref,
    dvalue_ref,
):
    step = pl.program_id(0)
    d = middle_ref.shape[1]

    @pl.when(step == 0)
    def _():
        keyval = dot_nn(partner_ref[...], project_ref[:, d:]).astype(BF16)
        key_ref[...] = keyval[:, :d]
        value_ref[...] = keyval[:, d:]
        for ref in (
            dkey_ref,
            dvalue_ref,
            g_project_ref,
            g_merge_ref,
            g_in_ref,
            g_out_ref,
            g_gain_ref,
        ):
            ref[...] = jnp.zeros(ref.shape, ref.dtype)

    middle = middle_ref[...]
    query = dot_nn(middle, project_ref[:, :d]).astype(BF16)
    keys = key_ref[...]
    values = value_ref[...]
    shares = softmax_rows(dot_nt(query, keys) * d**-0.5)
    weights = shares.astype(BF16)
    mix = dot_nn(weights, values).astype(BF16)
    unit_cross, inverse_cross = unit_norm(dot_nn(mix, merge_ref[...]))
    normed = (unit_cross * gains_ref[1:2, :]).astype(BF16)
    joined = jnp.concatenate([middle, normed], axis=1)
    pre = dot_nn(joined, feed_in_ref[...])
    bell = 0.5 * (1.0 + lax.erf(pre * HALF_ROOT))
    hidden = (pre * bell).astype(BF16)
    slope = bell + pre * jnp.exp(-0.5 * pre * pre) * DENSITY_COEF
    unit_feed, inverse_feed = unit_norm(dot_nn(hidden, feed_out_ref[...]))
    result_ref[...] = (middle.astype(F32) + unit_feed * gains_ref[2:3, :]).astype(BF16)
    upstream = upstream_ref[...]
    post = norm_backward(upstream, gains_ref[2:3, :], unit_feed, inverse_feed).astype(BF16)
    g_gain_ref[1:2, :] += jnp.sum(upstream * unit_feed, axis=0, keepdims=True) * scale
    grad_pre = (dot_nt(post, feed_out_ref[...]) * slope).astype(BF16)
    grad_joined = dot_nt(grad_pre, feed_in_ref[...])
    g_in_ref[...] += dot_tn(joined, grad_pre) * scale
    g_out_ref[...] += dot_tn(hidden, post) * scale
    grad_normed = grad_joined[:, d:]
    merged = norm_backward(grad_normed, gains_ref[1:2, :], unit_cross, inverse_cross).astype(BF16)
    g_gain_ref[0:1, :] += jnp.sum(grad_normed * unit_cross, axis=0, keepdims=True) * scale
    g_merge_ref[...] += dot_tn(mix, merged) * scale
    grad_mix = dot_nt(merged, merge_ref[...]).astype(BF16)
    portion = dot_nt(grad_mix, values)
    inner = jnp.sum(portion * shares, axis=-1, keepdims=True)
    scores = (shares * (portion - inner) * d**-0.5).astype(BF16)
    dvalue_ref[...] += dot_tn(weights, grad_mix)
    dkey_ref[...] += dot_tn(scores, query)
    grad_query = dot_nn(scores, keys).astype(BF16)
    g_project_ref[:, :d] += dot_tn(middle, grad_query) * scale
    partial_ref[...] = (
        upstream + grad_joined[:, :d] + dot_nt(grad_query, project_ref[:, :d])
    )

    @pl.when(step == pl.num_programs(0) - 1)
    def _():
        grad_kv = jnp.concatenate(
            [dkey_ref[...].astype(BF16), dvalue_ref[...].astype(BF16)], axis=1
        )
        term_ref[...] = dot_nt(grad_kv, project_ref[:, d:]).astype(BF16)
        g_project_ref[:, d:] = dot_tn(partner_ref[...], grad_kv) * scale


def merge_backward_kernel(
    scale,
    partial_ref,
    term_ref,
    mix_ref,
    merge_ref,
    gains_ref,
    middle_grad_ref,
    mix_grad_ref,
    g_merge_ref,
    g_gain_ref,
):
    @pl.when(pl.program_id(0) == 0)
    def _():
        g_merge_ref[...] = jnp.zeros(g_merge_ref.shape, F32)
        g_gain_ref[...] = jnp.zeros(g_gain_ref.shape, F32)

    grad = partial_ref[...] + term_ref[...].astype(F32)
    mix = mix_ref[...]
    unit, inverse = unit_norm(dot_nn(mix, merge_ref[...]))
    merged = norm_backward(grad, gains_ref[0:1, :], unit, inverse).astype(BF16)
    g_gain_ref[0:1, :] += jnp.sum(grad * unit, axis=0, keepdims=True) * scale
    g_merge_ref[...] += dot_tn(mix, merged) * scale
    middle_grad_ref[...] = grad
    mix_grad_ref[...] = dot_nt(merged, merge_ref[...]).astype(BF16)


def self_backward_kernel(
    cols,
    scale,
    valid_ref,
    own_ref,
    halo_ref,
    own_grad_ref,
    halo_grad_ref,
    middle_grad_ref,
    weight_ref,
    grad_ref,
    g_weight_ref,
):
    @pl.when(pl.program_id(0) == 0)
    def _():
        g_weight_ref[...] = jnp.zeros(g_weight_ref.shape, F32)

    d = own_ref.shape[1]
    count = own_ref.shape[0]
    flag = valid_ref[pl.program_id(0) // cols]
    own = own_ref[...]
    proj = dot_nn(jnp.concatenate([own, halo_ref[...]], axis=0), weight_ref[...]).astype(BF16)
    queries = proj[:, :d]
    keys = proj[:, d : 2 * d]
    values = proj[:, 2 * d :]
    halo_grad = jnp.where(flag > 0, halo_grad_ref[...].astype(F32), 0.0).astype(BF16)
    mix_grad = jnp.concatenate([own_grad_ref[...], halo_grad], axis=0)
    logits = dot_nt(queries, keys) * d**-0.5
    logits = jnp.where(window_keep(valid_ref, cols, count, 2 * count), logits, MASK_FILL)
    shares = softmax_rows(logits)
    portion = dot_nt(mix_grad, values)
    inner = jnp.sum(portion * shares, axis=-1, keepdims=True)
    scores = (shares * (portion - inner) * d**-0.5).astype(BF16)
    grad_query = dot_nn(scores[:count], keys)
    grad_key = dot_tn(scores[:, :count], queries)
    grad_value = dot_tn(shares[:, :count].astype(BF16), mix_grad)
    grad_proj = jnp.concatenate(
        [grad_query.astype(BF16), grad_key.astype(BF16), grad_value.astype(BF16)], axis=1
    )
    grad_ref[...] = middle_grad_ref[...] + dot_nt(grad_proj, weight_ref[...])
    g_weight_ref[...] += dot_tn(own, grad_proj) * scale


def rows_spec(rows, d):
    return pl.BlockSpec((rows, d), lambda i: (i, 0))


def whole_spec(array):
    return pl.BlockSpec(array.shape, lambda i: (0, 0))


SMEM_SPEC = pl.BlockSpec(memory_space=pltpu.SMEM)


def call(kernel, grid, in_specs, outs, scratch, flops, args):
    return pl.pallas_call(
        kernel,
        grid=(grid,),
        in_specs=in_specs,
        out_specs=[spec for spec, _ in outs],
        out_shape=[shape for _, shape in outs],
        scratch_shapes=scratch,
        compiler_params=pltpu.CompilerParams(
            dimension_semantics=("arbitrary",), vmem_limit_bytes=VMEM_BYTES
        ),
        cost_estimate=pl.CostEstimate(flops=flops, bytes_accessed=4_000_000, transcendentals=0),
    )(*args)


def tokens_out(rows, tokens, d, kind):
    return (rows_spec(rows, d), jax.ShapeDtypeStruct((tokens, d), kind))


def total_out(rows, columns):
    return (
        pl.BlockSpec((rows, columns), lambda i: (0, 0)),
        jax.ShapeDtypeStruct((rows, columns), F32),
    )


def to_windows(array, offset, cols):
    rows, width, d = array.shape
    half = rows // 2
    rolled = jnp.roll(array, -offset, axis=1).reshape(2, half, cols, WIN, d)
    return rolled.transpose(0, 2, 1, 3, 4).reshape(rows * width, d)


def from_windows(array, offset, cols, rows, width):
    d = array.shape[-1]
    half = rows // 2
    shaped = array.reshape(2, cols, half, WIN, d).transpose(0, 2, 1, 3, 4)
    return jnp.roll(shaped.reshape(rows, width, d), offset, axis=1)


def scatter_sum(arrays):
    count = lax.axis_size("tiles")
    flat = [a.reshape(count, -1) for a in arrays]
    joined = jnp.concatenate(flat, axis=1).astype(BF16)
    parts = lax.all_to_all(joined, "tiles", split_axis=0, concat_axis=0, tiled=True)
    total = jnp.sum(parts.astype(F32), axis=0)
    pieces = []
    start = 0
    for a in arrays:
        size = a.size // count
        pieces.append(total[start : start + size].reshape(a.shape[0] // count, -1))
        start += size
    return pieces


def body(
    features,
    window_offsets,
    self_project,
    self_merge,
    cross_project,
    cross_merge,
    feed_in,
    feed_out,
    norm_gains,
    result_grad,
):
    rows, width, d = features.shape
    hidden = feed_in.shape[1]
    tokens = rows * width
    half_tokens = tokens // 2
    cols = width // WIN
    windows = 2 * cols
    per_window = tokens // windows
    count = lax.axis_size("tiles")
    half_tiles = count // 2
    position = lax.axis_index("tiles")
    place = (position + count - count // 4) % count
    offset = window_offsets[place // half_tiles]
    scale = 1.0 / math.sqrt(count * tokens)
    valid = jnp.stack(
        [place % half_tiles != 0, place % half_tiles != half_tiles - 1]
    ).astype(jnp.int32)

    own = to_windows(features, offset, cols)

    def halo_of(array):
        above = passed_along(array[half_tokens:], "tiles", 1)
        below = passed_along(array[:half_tokens], "tiles", -1)
        return jnp.concatenate([above, below], axis=0)

    halo = halo_of(own)
    upstream = to_windows(result_grad, offset, cols)
    window_spec = rows_spec(per_window, d)
    self_mix, middle = call(
        functools.partial(self_forward_kernel, cols),
        windows,
        [
            SMEM_SPEC,
            window_spec,
            window_spec,
            whole_spec(self_project),
            whole_spec(self_merge),
            whole_spec(norm_gains),
        ],
        [tokens_out(per_window, tokens, d, BF16), tokens_out(per_window, tokens, d, BF16)],
        [],
        2_000_000_000,
        (valid, own, halo, self_project, self_merge, norm_gains),
    )
    partner = passed_along(middle, "tiles", half_tiles)
    block = min(256, tokens)
    block_spec = rows_spec(block, d)
    result, partial, term, g_cross, g_cross_merge, g_in, g_out, g_gain = call(
        functools.partial(cross_kernel, scale),
        tokens // block,
        [
            block_spec,
            whole_spec(partner),
            block_spec,
            whole_spec(cross_project),
            whole_spec(cross_merge),
            whole_spec(feed_in),
            whole_spec(feed_out),
            whole_spec(norm_gains),
        ],
        [
            tokens_out(block, tokens, d, BF16),
            tokens_out(block, tokens, d, F32),
            (
                pl.BlockSpec((tokens, d), lambda i: (0, 0)),
                jax.ShapeDtypeStruct((tokens, d), BF16),
            ),
            total_out(d, 3 * d),
            total_out(d, d),
            total_out(2 * d, hidden),
            total_out(hidden, d),
            total_out(2, d),
        ],
        [
            pltpu.VMEM((tokens, d), BF16),
            pltpu.VMEM((tokens, d), BF16),
            pltpu.VMEM((tokens, d), F32),
            pltpu.VMEM((tokens, d), F32),
        ],
        14_000_000_000,
        (middle, partner, upstream, cross_project, cross_merge, feed_in, feed_out, norm_gains),
    )
    returned = passed_along(term, "tiles", half_tiles)
    s_in, s_out, s_cross, s_cross_merge = scatter_sum([g_in, g_out, g_cross, g_cross_merge])
    result = from_windows(result, offset, cols, rows, width)
    middle_grad, mix_grad, g_merge, g_gain_self = call(
        functools.partial(merge_backward_kernel, scale),
        tokens // block,
        [
            block_spec,
            block_spec,
            block_spec,
            whole_spec(self_merge),
            whole_spec(norm_gains),
        ],
        [
            tokens_out(block, tokens, d, F32),
            tokens_out(block, tokens, d, BF16),
            total_out(d, d),
            total_out(1, d),
        ],
        [],
        400_000_000,
        (partial, returned, self_mix, self_merge, norm_gains),
    )
    halo_grad = halo_of(mix_grad)
    grad_windows, g_self = call(
        functools.partial(self_backward_kernel, cols, scale),
        windows,
        [
            SMEM_SPEC,
            window_spec,
            window_spec,
            window_spec,
            window_spec,
            window_spec,
            whole_spec(self_project),
        ],
        [tokens_out(per_window, tokens, d, F32), total_out(d, 3 * d)],
        [],
        5_000_000_000,
        (valid, own, halo, mix_grad, halo_grad, middle_grad, self_project),
    )
    gains = jnp.concatenate([g_gain_self, g_gain], axis=0)
    gains = gains.reshape(3, count, d // count).transpose(1, 0, 2).reshape(count, -1)
    s_self, s_merge, s_gains = scatter_sum([g_self, g_merge, gains])
    features_grad = from_windows(grad_windows, offset, cols, rows, width)
    return (
        result,
        features_grad,
        s_self.reshape(d // count, 3 * d),
        s_merge.reshape(d // count, d),
        s_cross.reshape(d // count, 3 * d),
        s_cross_merge.reshape(d // count, d),
        s_in.reshape(2 * d // count, hidden),
        s_out.reshape(hidden // count, d),
        s_gains.reshape(3, d // count),
    )


def solution(mesh):
    rows3 = P(("groups", "tiles"), None, None)
    rows2 = P(("groups", "tiles"), None)
    return jax.shard_map(
        body,
        mesh=mesh,
        in_specs=(rows3, P("groups")) + (P(),) * 7 + (rows3,),
        out_specs=(rows3, rows3) + (rows2,) * 6 + (P("groups", "tiles"),),
        check_vma=False,
    )
```

time: 492 us -> 182 us (0.37)
  waiting for transfers between devices: 238 us -> 52.2 us
  matrix products: 112 us -> 0 us
  Pallas kernels: 0 us -> 72.4 us
  blocking collectives: 29.6 us -> 0 us
  other arithmetic: 44.1 us -> 16.5 us
  local copies, waits for them, and re-layouts: 33.3 us -> 16.9 us
  between operations: 18.5 us -> 3.67 us
  starting transfers between devices: 11.4 us -> 19.4 us
    reduce_scatter x2 -> x0, waiting for transfers between devices: 114 us -> none  [the longest x1 59 us: body(): lax.psum_scatter(grad_feed_in, 'tiles', scatter_dimension=0, tiled=True)]
    dot_general x55 -> x0, matrix products: 112 us -> none  [the longest x5 27.6 us: shares_backward(): jnp.einsum('nvw,nvc->nwc', logit_gradient, query_rows, preferred_element_...]
    pallas_call x0 -> x4, Pallas kernels: none -> 72.4 us  [call(): pl.pallas_call(kernel, grid=(grid,), in_specs=in_specs, out_specs=[spec f...]
    unnamed x4 -> x0, waiting for transfers between devices: 49.5 us -> none
    unnamed x1 -> x0, blocking collectives: 29.6 us -> none
    ppermute x4 -> x6, waiting for transfers between devices: 71.7 us -> 48.4 us  [passed_along(): lax.ppermute(array, axis, [(i, (i + by) % length) for i in range(length)])]
    convert_element_type x9 -> x1, other arithmetic: 14.6 us -> 0.58 us  [body(): valid = jnp.stack([place % half_tiles != 0, place % half_tiles != half_ti...]
    all_to_all x0 -> x2, starting transfers between devices: none -> 12 us  [scatter_sum(): lax.all_to_all(joined, 'tiles', split_axis=0, concat_axis=0, tiled=True)]
  transfers between devices with their start and end apart: 9 -> 8, of which waited for: 6 -> 4; matrix products, arithmetic and copies ran while one was open for 9% -> 13% of each run, Pallas kernels for 0% -> 8%
where the time goes in v1:
time: 182 us; the launch traced here: 181 us
  Pallas kernels  72.4 us (40%)
  waiting for transfers between devices  52.2 us (29%)
  starting transfers between devices  19.4 us (11%)
  local copies, waits for them, and re-layouts  16.9 us (9%)
  other arithmetic  16.5 us (9%)
  between operations  3.67 us (2%)
    pallas_call x4, Pallas kernels, call(): pl.pallas_call(kernel, grid=(grid,), in_specs=in_specs, out_specs=[spec f...  72.4 us
    ppermute x6, waiting for transfers between devices, passed_along(): lax.ppermute(array, axis, [(i, (i + by) % length) for i in range(length)])  48.4 us
    all_to_all x2, starting transfers between devices, scatter_sum(): lax.all_to_all(joined, 'tiles', split_axis=0, concat_axis=0, tiled=True)  12 us
    ppermute x6, starting transfers between devices, passed_along(): lax.ppermute(array, axis, [(i, (i + by) % length) for i in range(length)])  7.49 us
    concatenate x4, other arithmetic, scatter_sum(): joined = jnp.concatenate(flat, axis=1).astype(BF16)  6.66 us
    unnamed x25, local copies, waits for them, and re-layouts  5.73 us
    all_to_all x2, waiting for transfers between devices, scatter_sum(): lax.all_to_all(joined, 'tiles', split_axis=0, concat_axis=0, tiled=True)  3.84 us
  transfers between devices with their start and end apart: 8, of which 4 were waited for; matrix products, arithmetic and copies ran while one was open for 13% of the time, Pallas kernels for 8%

profile of v1, /device:TPU:0, one launch (start us, length us, event | category | flops | bytes accessed | tf_op | source)
XLA Modules:
  0.0 181.1 jit_solution(11794170488824712018)
XLA Ops:
  0.7 1.2 dynamic_slice.9
  3.2 1.4 fusion.3
  5.2 5.1 %collective-permute-start.1 = (bf16[1024,128]{1,0:T(8,128)(2,1)S(1)}, bf16[1024,128]{1,0:T(8,128)(2,1)S(1)}, u32[]{:S(2)}, u32[]{:S(2)}) collective-permute-start(bf16[1024,128]{1,0:T(8,128)(2,1)S(1)} %bitcast.40), channel_id=1, source_target_pairs={{0,15},{1,0},{2,1},{3,2},{4,3},{5,4},{6,5},{7,6},{8,7},{9,8},{10,9... | collective-permute-start | bytes 786440 | tf_op jit(solution)/shard_map/ppermute | solution.py:23
  10.3 0.9 copy.30
  11.8 2.6 %collective-permute-done = bf16[1024,128]{1,0:T(8,128)(2,1)S(1)} collective-permute-done((bf16[1024,128]{1,0:T(8,128)(2,1)S(1)}, bf16[1024,128]{1,0:T(8,128)(2,1)S(1)}, u32[]{:S(2)}, u32[]{:S(2)}) %collective-permute-start) | collective-permute-done | bytes 262176 | tf_op jit(solution)/shard_map/ppermute | solution.py:23
  15.3 10.6 %shard_map.169 = (bf16[2048,128]{1,0:T(8,128)(2,1)}, bf16[2048,128]{1,0:T(8,128)(2,1)}) custom-call(s32[2]{0:T(128)} %add_convert_fusion.valid_ref, bf16[2048,128]{1,0:T(8,128)(2,1)} %bitcast.36, bf16[2048,128]{1,0:T(8,128)(2,1)} %copy-done.5, bf16[128,384]{1,0:T(8,128)(2,1)} %weight_ref.3, bf16[128,128]{1,0:T(8,128)(2,1)} %merge_ref.5, f32[3,128]{1,0:T(4,128)} %gains_ref.5), custom_call_target="tpu_custom_call" | custom-call | flops 2000000000 | bytes 4000000 | tf_op jit(solution)/shard_map/pallas_call | solution.py:256
  25.9 1.2 collective-permute-start.2
  27.4 1.1 copy.33
  28.4 24.1 %collective-permute-done.2.partner_ref = bf16[2048,128]{1,0:T(8,128)(2,1)S(1)} collective-permute-done((bf16[2048,128]{1,0:T(8,128)(2,1)}, bf16[2048,128]{1,0:T(8,128)(2,1)S(1)}, u32[]{:S(2)}, u32[]{:S(2)}) %collective-permute-start.2) | collective-permute-done | bytes 524320 | tf_op jit(solution)/shard_map/ppermute | solution.py:23
  52.6 0.8 copy-done.7
  53.4 40.6 %shard_map.170 = (bf16[2048,128]{1,0:T(8,128)(2,1)}, f32[2048,128]{1,0:T(8,128)}, bf16[2048,128]{1,0:T(8,128)(2,1)}, f32[128,384]{1,0:T(8,128)}, f32[128,128]{1,...) custom-call(bf16[2048,128]{1,0:T(8,128)(2,1)} %get-tuple-element.27.middle_ref, ...), custom_call_target="tpu_custom_call" | custom-call | flops 14000000000 | bytes 4000000 | tf_op jit(solution)/shard_map/pallas_call | solution.py:256
  95.4 0.8 convert.41
  96.3 0.9 convert.40
  97.2 1.0 convert.39
  98.5 21.6 %collective-permute-done.3.term_ref = bf16[2048,128]{1,0:T(8,128)(2,1)S(1)} collective-permute-done((bf16[2048,128]{1,0:T(8,128)(2,1)}, bf16[2048,128]{1,0:T(8,128)(2,1)S(1)}, u32[]{:S(2)}, u32[]{:S(2)}) %collective-permute-start.3) | collective-permute-done | bytes 524320 | tf_op jit(solution)/shard_map/ppermute | solution.py:23
  120.2 0.8 copy-done.1
  121.0 7.6 %shard_map.171 = (f32[2048,128]{1,0:T(8,128)}, bf16[2048,128]{1,0:T(8,128)(2,1)}, f32[128,128]{1,0:T(8,128)}, f32[1,128]{1,0:T(1,128)}) custom-call(f32[2048,128]{1,0:T(8,128)} %get-tuple-element.29.partial_ref, bf16[2048,128]{1,0:T(8,128)(2,1)} %copy-done.1, bf16[2048,128]{1,0:T(8,128)(2,1)} %get-tuple-element.31.mix_ref, bf16[128,128]{1,0:T(8,128)(2,1)} %merge_ref.5, ...), custom_call_target="tpu_custom_call" | custom-call | flops 400000000 | bytes 4000000 | tf_op jit(solution)/shard_map/pallas_call | solution.py:256
  128.5 1.1 fusion.4
  130.2 1.1 pad_maximum_fusion
  132.6 3.8 %reduce.3 = bf16[16,16384]{1,0:T(8,128)(2,1)S(1)} reduce(bf16[16,1,16384]{2,1,0:T(2,128)(2,1)S(1)} %pad_maximum_fusion, bf16[]{:T(256)} %broadcast.5), dimensions={1}, to_apply=%pad_maximum_fusion.reduce_sub_computation | reduce | bytes 1048578 | tf_op jit(solution)/shard_map/concatenate | solution.py:298
  136.4 1.2 reshape.230
  137.6 6.0 %all-to-all-start.1 = ((bf16[16,2,8192]{2,1,0:T(2,128)(2,1)}), bf16[16,2,8192]{2,1,0:T(2,128)(2,1)S(1)}, u32[]{:S(2)}, u32[]{:S(2)}) async-start(bf16[16,2,8192]{2,1,0:T(2,128)(2,1)} %reshape.230), calls=%async_computation.1 | async-start | bytes 1048576 | tf_op jit(solution)/shard_map/all_to_all | solution.py:299
  143.5 1.2 fusion.2
  145.0 0.8 pad_maximum_fusion.1.halo_grad_ref
  145.9 13.6 %shard_map.172 = (f32[2048,128]{1,0:T(8,128)}, f32[128,384]{1,0:T(8,128)}) custom-call(s32[2]{0:T(128)} %add_convert_fusion.valid_ref, bf16[2048,128]{1,0:T(8,128)(2,1)} %bitcast.37, bf16[2048,128]{1,0:T(8,128)(2,1)} %copy-done.5, bf16[2048,128]{1,0:T(8,128)(2,1)} %get-tuple-element.32.own_grad_ref, bf16[2048,128]{1,0:T(8,128)(2,1)} %pad_maximum_fusion.1.halo_grad_ref, ...), custom_call_target="tpu_custom_call" | custom-call | flops 5000000000 | bytes 4000000 | tf_op jit(solution)/shard_map/pallas_call | solution.py:256
  159.5 1.3 copy.35
  161.3 1.5 reduce.2
  162.7 0.8 reshape.228
  163.5 1.2 fusion
  164.7 6.0 %all-to-all-start = ((bf16[16,2,2060]{2,1,0:T(2,128)(2,1)}), bf16[16,2,2060]{2,1,0:T(2,128)(2,1)S(1)}, u32[]{:S(2)}, u32[]{:S(2)}) async-start(bf16[16,2,2060]{2,1,0:T(2,128)(2,1)} %reshape.228), calls=%async_computation | async-start | bytes 278528 | tf_op jit(solution)/shard_map/all_to_all | solution.py:299
  171.3 1.2 convert_reduce_fusion
  175.0 3.8 %all-to-all-done = bf16[16,2,2060]{2,1,0:T(2,128)(2,1)S(1)} async-done(((bf16[16,2,2060]{2,1,0:T(2,128)(2,1)}), bf16[16,2,2060]{2,1,0:T(2,128)(2,1)S(1)}, u32[]{:S(2)}, u32[]{:S(2)}) %all-to-all-start) | async-done | bytes 131872 | tf_op jit(solution)/shard_map/all_to_all | solution.py:299
  (65 shorter events, 10.4 us)
Async XLA Ops:
  4.7 9.7 %collective-permute-start = (bf16[1024,128]{1,0:T(8,128)(2,1)S(1)}, bf16[1024,128]{1,0:T(8,128)(2,1)S(1)}, u32[]{:S(2)}, u32[]{:S(2)}) collective-permute-start(bf16[1024,128]{1,0:T(8,128)(2,1)S(1)} %bitcast.39), channel_id=1, source_target_pairs={{0,1},{1,2},{2,3},{3,4},{4,5},{5,6},{6,7},{7,8},{8,9},{9,10},{10,1... | collective-permute-start | bytes 786440 | tf_op jit(solution)/shard_map/ppermute | solution.py:23
  5.2 9.2 %collective-permute-start.1 = (bf16[1024,128]{1,0:T(8,128)(2,1)S(1)}, bf16[1024,128]{1,0:T(8,128)(2,1)S(1)}, u32[]{:S(2)}, u32[]{:S(2)}) collective-permute-start(bf16[1024,128]{1,0:T(8,128)(2,1)S(1)} %bitcast.40), channel_id=1, source_target_pairs={{0,15},{1,0},{2,1},{3,2},{4,3},{5,4},{6,5},{7,6},{8,7},{9,8},{10,9... | collective-permute-start | bytes 786440 | tf_op jit(solution)/shard_map/ppermute | solution.py:23
  14.5 0.8 copy-start.5
  15.2 11.8 %copy-start = (f32[16,128,128]{2,1,0:T(8,128)S(1)}, f32[16,128,128]{2,1,0:T(8,128)}, u32[]{:S(2)}) copy-start(f32[16,128,128]{2,1,0:T(8,128)} %param.23) | copy-start | bytes 3145732
  25.9 26.7 %collective-permute-start.2 = (bf16[2048,128]{1,0:T(8,128)(2,1)}, bf16[2048,128]{1,0:T(8,128)(2,1)S(1)}, u32[]{:S(2)}, u32[]{:S(2)}) collective-permute-start(bf16[2048,128]{1,0:T(8,128)(2,1)} %get-tuple-element.27.middle_ref), channel_id=1, source_target_pairs={{0,8},{1,9},{2,10},{3,11},{4,12},{5,13},{6,14},{7,15},{8,0},{9,1},... | collective-permute-start | bytes 1572872 | tf_op jit(solution)/shard_map/ppermute | solution.py:23
  52.6 0.8 copy-start.7
  94.0 4.3 %copy-start.2 = (f32[256,512]{1,0:T(8,128)S(1)}, f32[256,512]{1,0:T(8,128)}, u32[]{:S(2)}) copy-start(f32[256,512]{1,0:T(8,128)} %get-tuple-element.39) | copy-start | bytes 1572868
  94.0 26.2 %collective-permute-start.3 = (bf16[2048,128]{1,0:T(8,128)(2,1)}, bf16[2048,128]{1,0:T(8,128)(2,1)S(1)}, u32[]{:S(2)}, u32[]{:S(2)}) collective-permute-start(bf16[2048,128]{1,0:T(8,128)(2,1)} %get-tuple-element.30), channel_id=1, source_target_pairs={{0,8},{1,9},{2,10},{3,11},{4,12},{5,13},{6,14},{7,15},{8,0},{9,1},... | collective-permute-start | bytes 1572872 | tf_op jit(solution)/shard_map/ppermute | solution.py:23
  120.2 0.8 copy-start.1
  129.6 15.4 %collective-permute-start.5 = (bf16[1024,128]{1,0:T(8,128)(2,1)S(1)}, bf16[1024,128]{1,0:T(8,128)(2,1)S(1)}, u32[]{:S(2)}, u32[]{:S(2)}) collective-permute-start(bf16[1024,128]{1,0:T(8,128)(2,1)S(1)} %get-tuple-element.44), channel_id=1, source_target_pairs={{0,15},{1,0},{2,1},{3,2},{4,3},{5,4},{6,5},{7,6},{8,7},{9,8},{10,9... | collective-permute-start | bytes 786440 | tf_op jit(solution)/shard_map/ppermute | solution.py:23
  130.2 1.2 copy-start.3
  130.2 14.8 %collective-permute-start.4 = (bf16[1024,128]{1,0:T(8,128)(2,1)S(1)}, bf16[1024,128]{1,0:T(8,128)(2,1)S(1)}, u32[]{:S(2)}, u32[]{:S(2)}) collective-permute-start(bf16[1024,128]{1,0:T(8,128)(2,1)S(1)} %get-tuple-element.43), channel_id=1, source_target_pairs={{0,1},{1,2},{2,3},{3,4},{4,5},{5,6},{6,7},{7,8},{8,9},{9,10},{10,1... | collective-permute-start | bytes 786440 | tf_op jit(solution)/shard_map/ppermute | solution.py:23
  131.4 0.7 copy-start.9
  137.6 7.1 %copy-start.8 = (f32[1,128]{1,0:T(1,128)S(1)}, f32[1,128]{1,0:T(1,128)}, u32[]{:S(2)}) copy-start(f32[1,128]{1,0:T(1,128)} %get-tuple-element.37) | copy-start | bytes 1540
  137.6 7.4 %copy-start.6 = (f32[128,128]{1,0:T(8,128)S(1)}, f32[128,128]{1,0:T(8,128)}, u32[]{:S(2)}) copy-start(f32[128,128]{1,0:T(8,128)} %get-tuple-element.36) | copy-start | bytes 196612
  137.6 27.2 %all-to-all-start.1 = ((bf16[16,2,8192]{2,1,0:T(2,128)(2,1)}), bf16[16,2,8192]{2,1,0:T(2,128)(2,1)S(1)}, u32[]{:S(2)}, u32[]{:S(2)}) async-start(bf16[16,2,8192]{2,1,0:T(2,128)(2,1)} %reshape.230), calls=%async_computation.1 | async-start | bytes 1048576 | tf_op jit(solution)/shard_map/all_to_all | solution.py:299
  159.5 1.4 copy-start.4
  164.7 14.1 %all-to-all-start = ((bf16[16,2,2060]{2,1,0:T(2,128)(2,1)}), bf16[16,2,2060]{2,1,0:T(2,128)(2,1)S(1)}, u32[]{:S(2)}, u32[]{:S(2)}) async-start(bf16[16,2,2060]{2,1,0:T(2,128)(2,1)} %reshape.228), calls=%async_computation | async-start | bytes 278528 | tf_op jit(solution)/shard_map/all_to_all | solution.py:299
